TPU v7x, 1024 devices: a whole 4x4x32 slice. The times are simulated.
1024 devices in a mesh: dp: 32 (over y, x, core), ctx: 32 (over z).
Axes of the slice: x: 4, y: 4, z: 32, core: 2. Of those that a mesh axis runs over, the one named last changes fastest.
Arguments:
- queries: bfloat16 [131072, 2048], P(('dp', 'ctx')), may hold values from -120 to 120
- keys: bfloat16 [131072, 512], P(('dp', 'ctx')), may hold values from -5.5 to 5.5
- values: bfloat16 [131072, 512], P(('dp', 'ctx')), may hold values from -6 to 6
- output_gradient: bfloat16 [131072, 2048], P(('dp', 'ctx')), may hold values from -6 to 6
- doc_blocks: int32 [512], P('dp'), may hold values from 1 to 3, 1024 in all
- doc_pad: int32 [512], P('dp'), may hold values from 0 to 127
Outputs:
- attn_out: bfloat16 [131072, 2048], P(('dp', 'ctx'))
- grad_queries: bfloat16 [131072, 2048], P(('dp', 'ctx'))
- grad_keys: bfloat16 [131072, 512], P(('dp', 'ctx'))
- grad_values: bfloat16 [131072, 512], P(('dp', 'ctx'))
All inputs are finite; a program needn't handle non-finite values. No bound on the sum of `doc_blocks` on one device may be relied on, other than what follows from the above.
Results may differ from a plain program's by a relative error of at most 0.02.
Values may be sent and summed in bfloat16 or wider, within the bound.
A program may use at most 32 MiB of HBM per device.

v0:
```python
import jax
import jax.numpy as jnp
from jax import lax
from jax.sharding import PartitionSpec as P

QUERY_HEADS = 16
KEY_VALUE_HEADS = 4
HEAD_SIZE = 128
MOST_DOC_BLOCKS = 3


def passed_along(array, axis, by):
    count = lax.axis_size(axis)
    pairs = [(i, i + by) for i in range(count) if 0 <= i + by < count]
    return lax.ppermute(array, axis, pairs)


def entering(array, axis, combine, identity):
    count, place = (lax.axis_size(axis), lax.axis_index(axis))
    everything = lax.all_gather(array, axis)
    start = jnp.broadcast_to(jnp.asarray(identity, array.dtype), array.shape)

    def lap(k, before):
        reached = k < place
        new = combine(before, everything[k])
        return jnp.where(reached, new, before)

    return lax.fori_loop(0, count, lap, start)


def block_meta(block_ids, starts, doc_sizes, doc_pads, token_rows, block_count):
    in_range = (block_ids >= 0) & (block_ids < block_count)
    doc_index = jnp.sum((starts[None, :] <= block_ids[:, None]).astype(jnp.int32), axis=1) - 1
    doc_index = jnp.where(in_range, doc_index, -1)
    one_hot = jnp.arange(starts.shape[0], dtype=jnp.int32)[None, :] == doc_index[:, None]
    doc_ends = jnp.sum(
        jnp.where(one_hot, (starts + doc_sizes)[None, :] * token_rows - doc_pads[None, :], 0),
        axis=1,
    )
    positions = block_ids[:, None] * token_rows + jnp.arange(token_rows, dtype=jnp.int32)[None, :]
    is_valid = (positions < doc_ends[:, None]) & in_range[:, None]
    doc_ids = jnp.broadcast_to(doc_index[:, None], positions.shape)
    return (doc_ids.reshape(-1), positions.reshape(-1), is_valid.reshape(-1))


def allowed_pairs(query_info, key_info):
    same_doc = query_info[0][:, None] == key_info[0][None, :]
    causal = key_info[1][None, :] <= query_info[1][:, None]
    return same_doc & causal & query_info[2][:, None] & key_info[2][None, :]


def scores_of(query_rows, key_rows, score_scale):
    return (
        jnp.einsum("tkgd,skd->kgts", query_rows, key_rows, preferred_element_type=jnp.float32)
        * score_scale
    )


def softmax_parts(score_f32, pair_mask, query_valid):
    masked = jnp.where(pair_mask, score_f32, -jnp.inf)
    row_peak = jnp.where(query_valid, jnp.max(masked, axis=-1), 0.0)
    row_total = jnp.sum(
        jnp.where(pair_mask, jnp.exp(score_f32 - row_peak[..., None]), 0.0), axis=-1
    )
    log_total = row_peak + jnp.log(jnp.where(query_valid, row_total, 1.0))
    weight = jnp.where(pair_mask, jnp.exp(score_f32 - log_total[..., None]), 0.0)
    return (log_total, weight)


def fetch_back(payload, offset_step):
    return passed_along(payload, ("dp", "ctx"), offset_step)


def send_terms(payload, offset_step):
    return passed_along(payload, ("dp", "ctx"), offset_step)


def on_device(queries, keys, values, output_gradient, doc_blocks, doc_pad):
    token_rows = queries.shape[0]
    head_group_width = QUERY_HEADS // KEY_VALUE_HEADS
    score_scale = HEAD_SIZE ** (-0.5)
    backward_distance = MOST_DOC_BLOCKS - 1
    block_count = lax.axis_size("dp") * lax.axis_size("ctx")
    my_block = lax.axis_index("dp") * lax.axis_size("ctx") + lax.axis_index("ctx")
    local_total = jnp.sum(doc_blocks)
    before = entering(local_total, "dp", jnp.add, jnp.int32(0))
    local_starts = before + jnp.cumsum(doc_blocks) - doc_blocks
    starts, doc_sizes, doc_pads = (
        lax.all_gather(local_starts, "dp", axis=0, tiled=True),
        lax.all_gather(doc_blocks, "dp", axis=0, tiled=True),
        lax.all_gather(doc_pad, "dp", axis=0, tiled=True),
    )

    def meta(block_ids):
        return block_meta(block_ids, starts, doc_sizes, doc_pads, token_rows, block_count)

    single = my_block + jnp.zeros((1,), jnp.int32)
    span = jnp.arange(MOST_DOC_BLOCKS, dtype=jnp.int32)
    own_info = meta(single)
    pair_mask = allowed_pairs(own_info, meta(my_block - backward_distance + span))
    key_value = jnp.stack([keys, values])
    pieces = []
    for offset_step in range(backward_distance, 0, -1):
        pieces.append(fetch_back(key_value, offset_step))
    pieces.append(key_value)
    neighbor_key_values = jnp.concatenate(pieces, axis=1)
    neighbor_keys = neighbor_key_values[0].reshape(
        MOST_DOC_BLOCKS * token_rows, KEY_VALUE_HEADS, HEAD_SIZE
    )
    neighbor_values = neighbor_key_values[1].reshape(
        MOST_DOC_BLOCKS * token_rows, KEY_VALUE_HEADS, HEAD_SIZE
    )
    query_head_rows = queries.reshape(token_rows, KEY_VALUE_HEADS, head_group_width, HEAD_SIZE)
    gradient_heads = output_gradient.reshape(
        token_rows, KEY_VALUE_HEADS, head_group_width, HEAD_SIZE
    )
    score_f32 = scores_of(query_head_rows, neighbor_keys, score_scale)
    log_total, weight = softmax_parts(score_f32, pair_mask, own_info[2])
    weight_bf16 = weight.astype(jnp.bfloat16)
    attn = jnp.einsum(
        "kgts,skd->tkgd", weight_bf16, neighbor_values, preferred_element_type=jnp.float32
    ).astype(jnp.bfloat16)
    delta_rows = jnp.einsum(
        "tkgd,tkgd->kgt", gradient_heads, attn, preferred_element_type=jnp.float32
    )
    dprob = jnp.einsum(
        "tkgd,skd->kgts", gradient_heads, neighbor_values, preferred_element_type=jnp.float32
    )
    dscore = (weight * (dprob - delta_rows[..., None])).astype(jnp.bfloat16)
    grad_q = (
        jnp.einsum("kgts,skd->tkgd", dscore, neighbor_keys, preferred_element_type=jnp.float32)
        * score_scale
    )
    summand_keys = jnp.einsum(
        "kgts,tkgd->skd", dscore, query_head_rows, preferred_element_type=jnp.float32
    )
    summand_values = jnp.einsum(
        "kgts,tkgd->skd", weight_bf16, gradient_heads, preferred_element_type=jnp.float32
    )
    terms = jnp.stack([summand_keys, summand_values]).reshape(
        2, MOST_DOC_BLOCKS, token_rows, KEY_VALUE_HEADS * HEAD_SIZE
    )
    gathered = terms[:, backward_distance]
    for offset_step in range(1, backward_distance + 1):
        gathered = gathered + send_terms(terms[:, backward_distance - offset_step], -offset_step)
    grad_k = (gathered[0] * score_scale).astype(jnp.bfloat16)
    grad_v = gathered[1].astype(jnp.bfloat16)
    return (
        attn.reshape(token_rows, QUERY_HEADS * HEAD_SIZE),
        grad_q.astype(jnp.bfloat16).reshape(token_rows, QUERY_HEADS * HEAD_SIZE),
        grad_k,
        grad_v,
    )


def solution(mesh):
    in_specs = (
        P(("dp", "ctx"), None),
        P(("dp", "ctx"), None),
        P(("dp", "ctx"), None),
        P(("dp", "ctx"), None),
        P("dp"),
        P("dp"),
    )
    out_specs = (
        P(("dp", "ctx"), None),
        P(("dp", "ctx"), None),
        P(("dp", "ctx"), None),
        P(("dp", "ctx"), None),
    )
    return jax.shard_map(
        on_device, mesh=mesh, in_specs=in_specs, out_specs=out_specs, check_vma=False
    )
```

profile of v0, /device:TPU:25, one launch (start us, length us, event | category | flops | bytes accessed | tf_op | source)
XLA Modules:
  0.0 170.5 jit_solution(16147957364716695770)
XLA Ops:
  2.7 3.5 %collective-permute-start.1 = (bf16[2,128,512]{1,2,0:T(8,128)(2,1)S(1)}, bf16[2,128,512]{1,2,0:T(8,128)(2,1)S(1)}, u32[]{:S(2)}, u32[]{:S(2)}) collective-permute-start(bf16[2,128,512]{1,2,0:T(8,128)(2,1)S(1)} %pad_maximum_fusion), channel_id=1, source_target_pairs={{0,1},{1,2},{2,3},{3,4},{4,5},{5,6},{6,7},{7,8},{8,9},{9,10},{10,1... | collective-permute-start | bytes 786440 | tf_op jit(solution)/shard_map/ppermute | solution.py:15
  6.3 4.9 %collective-permute-start = (bf16[2,128,512]{1,2,0:T(8,128)(2,1)S(1)}, bf16[2,128,512]{1,2,0:T(8,128)(2,1)S(1)}, u32[]{:S(2)}, u32[]{:S(2)}) collective-permute-start(bf16[2,128,512]{1,2,0:T(8,128)(2,1)S(1)} %pad_maximum_fusion), channel_id=1, source_target_pairs={{0,2},{1,3},{2,4},{3,5},{4,6},{5,7},{6,8},{7,9},{8,10},{9,11},{10,... | collective-permute-start | bytes 786440 | tf_op jit(solution)/shard_map/ppermute | solution.py:15
  12.0 1.3 reduce_sum.54
  13.3 1.3 dynamic-slice
  15.3 1.3 dynamic-update-slice
  16.6 12.6 %all-reduce = s32[32]{0:T(128)S(1)} all-reduce(s32[32]{0:T(128)S(1)} %dynamic-update-slice), channel_id=1, replica_groups=mesh['dp'=32,'ctx'=32] {'dp'}, use_global_device_ids=true, to_apply=%add | all-reduce | flops 32 | bytes 256
  29.2 40.5 %while.13 = (s32[]{:T(128)}, s32[]{:T(128)}, s32[]{:T(128)}, s32[32]{0:T(128)S(1)}, s32[]{:T(128)}) while((s32[]{:T(128)}, s32[]{:T(128)}, s32[]{:T(128)}, s32[32]{0:T(128)S(1)}, s32[]{:T(128)}) %tuple.42), condition=%wide.region_2.3_spmd, body=%wide.region_1.2_spmd.sunk | while | flops 5 | bytes 115 | solution.py:28
  72.3 14.7 %all-reduce.4 = (s32[512]{0:T(512)S(1)}, s32[512]{0:T(512)S(1)}, s32[512]{0:T(512)S(1)}) all-reduce(s32[512]{0:T(512)S(1)} %dynamic-update-slice.3, s32[512]{0:T(512)S(1)} %subtract_dynamic-update-slice_fusion, s32[512]{0:T(512)S(1)} %dynamic-update-slice.2), channel_id=1, replica_groups=mesh['dp'=32,'ctx'=32] {'dp'}, use_global_device_ids=true, to_apply=%add.3 | all-reduce | flops 1536 | bytes 12288
  90.1 2.2 %reshape.183 = bf16[128,4,4,128]{3,2,1,0:T(4,128)(2,1)} reshape(bf16[128,2048]{1,0:T(8,128)(2,1)} %param.8) | data formatting | bytes 1048576 | tf_op jit(solution)/shard_map/reshape | solution.py:113
  92.3 2.2 %reshape.185 = bf16[128,4,4,128]{3,2,1,0:T(4,128)(2,1)} reshape(bf16[128,2048]{1,0:T(8,128)(2,1)} %param.11) | data formatting | bytes 1048576 | tf_op jit(solution)/shard_map/reshape | solution.py:114
  97.0 1.9 %bitcast_convert_fusion = (f32[4,4,128,128]{2,3,1,0:T(8,128)}, bf16[4,128,4,128]{3,1,2,0:T(8,128)(2,1)}) fusion(bf16[384,4,128,1]{0,2,3,1:T(8,128)(2,1)S(1)} %bitcast.116, f32[4,384,128,4]{2,1,3,0:T(8,128)S(1)} %get-tuple-element.116, f32[4,4,128]{2,1,0:T(4,128)S(1)} %log_add_fusion, pred[128,384]{0,1:T(8,128)(4,1)S(1)} %and_and_fusion), kind=kOutput, calls=%fused_computation.25 | convolution fusion | flops 204996608 | bytes 5169152 | tf_op jit(solution)/shard_map/kgts,skd->tkgd/dot_general | solution.py:120
  98.9 2.7 %copy.65 = f32[4,4,128,128]{3,1,0,2:T(4,128)} copy(f32[4,4,128,128]{2,3,1,0:T(8,128)} %get-tuple-element.117) | data formatting | bytes 2097152
  101.6 2.8 %convolution_bitcast_fusion = f32[384,4,128]{2,0,1:T(8,128)} fusion(bf16[128,4,4,128]{3,2,1,0:T(4,128)(2,1)} %reshape.185, f32[4,384,128,4]{2,1,3,0:T(8,128)S(1)} %get-tuple-element.116, f32[4,4,128]{2,1,0:T(4,128)S(1)} %log_add_fusion, pred[128,384]{0,1:T(8,128)(4,1)} %copy-done.7), kind=kOutput, calls=%fused_computation.15 | convolution fusion | flops 204472320 | bytes 4513792 | tf_op jit(solution)/shard_map/kgts,tkgd->skd/dot_general | solution.py:137
  104.4 1.6 multiply_reduce_fusion
  107.0 2.4 %fusion.1 = bf16[4,4,128,384]{2,3,1,0:T(8,128)(2,1)S(1)} fusion(f32[4,384,128,4]{2,1,3,0:T(8,128)S(1)} %get-tuple-element.116, bf16[384,4,128,1]{0,2,3,1:T(8,128)(2,1)} %bitcast.117, f32[4,4,128]{2,1,0:T(4,128)S(1)} %copy.66, f32[4,4,128]{2,1,0:T(4,128)S(1)} %log_add_fusion, pred[128,384]{0,1:T(8,128)(4,1)} %copy-done.7, bf16[128,4,4,128]{3,2,1,0:T(4,128)(2,1)} %reshape.185), kind=kOutput, calls=%fused_computation.2 | convolution fusion | flops 206045184 | bytes 5701632 | tf_op jit(solution)/shard_map/tkgd,skd->kgts/dot_general | solution.py:126
  112.1 1.4 copy.51
  113.5 2.5 %stack.22 = f32[1,3,128,512]{3,2,1,0:T(8,128)} reshape(f32[384,4,128]{2,1,0:T(4,128)} %copy.51) | data formatting | bytes 1572864 | tf_op jit(solution)/shard_map/stack | solution.py:140
  118.2 17.7 %collective-permute-start.3 = (f32[2,128,512]{2,1,0:T(8,128)}, f32[2,128,512]{2,1,0:T(8,128)}, u32[]{:S(2)}, u32[]{:S(2)}) collective-permute-start(f32[2,128,512]{2,1,0:T(8,128)} %get-tuple-element.112), channel_id=1, source_target_pairs={{2,0},{3,1},{4,2},{5,3},{6,4},{7,5},{8,6},{9,7},{10,8},{11,9},{12,... | collective-permute-start | bytes 1572872 | tf_op jit(solution)/shard_map/ppermute | solution.py:15
  135.9 3.4 %collective-permute-start.2 = (f32[2,128,512]{2,1,0:T(8,128)}, f32[2,128,512]{2,1,0:T(8,128)}, u32[]{:S(2)}, u32[]{:S(2)}) collective-permute-start(f32[2,128,512]{2,1,0:T(8,128)} %get-tuple-element.111), channel_id=1, source_target_pairs={{1,0},{2,1},{3,2},{4,3},{5,4},{6,5},{7,6},{8,7},{9,8},{10,9},{11,1... | collective-permute-start | bytes 1572872 | tf_op jit(solution)/shard_map/ppermute | solution.py:15
  139.3 2.0 %copy.54 = bf16[128,2048]{1,0:T(8,128)(2,1)} copy(bf16[128,2048]{0,1:T(8,128)(2,1)} %bitcast.114) | data formatting | bytes 1048576
  142.5 2.0 %copy.55 = bf16[128,2048]{1,0:T(8,128)(2,1)} copy(bf16[128,2048]{0,1:T(8,128)(2,1)} %bitcast.115) | data formatting | bytes 1048576
  144.6 14.2 %collective-permute-done.3 = f32[2,128,512]{2,1,0:T(8,128)} collective-permute-done((f32[2,128,512]{2,1,0:T(8,128)}, f32[2,128,512]{2,1,0:T(8,128)}, u32[]{:S(2)}, u32[]{:S(2)}) %collective-permute-start.3) | collective-permute-done | bytes 524320 | tf_op jit(solution)/shard_map/ppermute | solution.py:15
  158.8 9.1 %collective-permute-done.2 = f32[2,128,512]{2,1,0:T(8,128)} collective-permute-done((f32[2,128,512]{2,1,0:T(8,128)}, f32[2,128,512]{2,1,0:T(8,128)}, u32[]{:S(2)}, u32[]{:S(2)}) %collective-permute-start.2) | collective-permute-done | bytes 524320 | tf_op jit(solution)/shard_map/ppermute | solution.py:15
  167.9 1.3 fusion.11
  (94 shorter events, 37.5 us)
Async XLA Ops:
  2.7 92.0 %collective-permute-start.1 = (bf16[2,128,512]{1,2,0:T(8,128)(2,1)S(1)}, bf16[2,128,512]{1,2,0:T(8,128)(2,1)S(1)}, u32[]{:S(2)}, u32[]{:S(2)}) collective-permute-start(bf16[2,128,512]{1,2,0:T(8,128)(2,1)S(1)} %pad_maximum_fusion), channel_id=1, source_target_pairs={{0,1},{1,2},{2,3},{3,4},{4,5},{5,6},{6,7},{7,8},{8,9},{9,10},{10,1... | collective-permute-start | bytes 786440 | tf_op jit(solution)/shard_map/ppermute | solution.py:15
  6.3 88.5 %collective-permute-start = (bf16[2,128,512]{1,2,0:T(8,128)(2,1)S(1)}, bf16[2,128,512]{1,2,0:T(8,128)(2,1)S(1)}, u32[]{:S(2)}, u32[]{:S(2)}) collective-permute-start(bf16[2,128,512]{1,2,0:T(8,128)(2,1)S(1)} %pad_maximum_fusion), channel_id=1, source_target_pairs={{0,2},{1,3},{2,4},{3,5},{4,6},{5,7},{6,8},{7,9},{8,10},{9,11},{10,... | collective-permute-start | bytes 786440 | tf_op jit(solution)/shard_map/ppermute | solution.py:15
  94.5 1.0 copy-start.2
  94.7 2.2 %copy-start.7 = (pred[128,384]{0,1:T(8,128)(4,1)}, pred[128,384]{0,1:T(8,128)(4,1)S(1)}, u32[]{:S(2)}) copy-start(pred[128,384]{0,1:T(8,128)(4,1)S(1)} %and_and_fusion) | copy-start | bytes 147460
  95.0 2.0 %copy-start.6 = (bf16[1,384,512]{1,2,0:T(8,128)(2,1)}, bf16[1,384,512]{1,2,0:T(8,128)(2,1)S(1)}, u32[]{:S(2)}) copy-start(bf16[1,384,512]{1,2,0:T(8,128)(2,1)S(1)} %get-tuple-element.114) | copy-start | bytes 1179652
  101.6 2.8 %copy-start.4 = (f32[4,4,128,128]{3,1,0,2:T(4,128)S(1)}, f32[4,4,128,128]{3,1,0,2:T(4,128)}, u32[]{:S(2)}) copy-start(f32[4,4,128,128]{3,1,0,2:T(4,128)} %copy.65) | copy-start | bytes 3145732
  101.6 2.8 %copy-start.5 = (bf16[128,4,4,128]{3,2,1,0:T(4,128)(2,1)S(1)}, bf16[128,4,4,128]{3,2,1,0:T(4,128)(2,1)}, u32[]{:S(2)}) copy-start(bf16[128,4,4,128]{3,2,1,0:T(4,128)(2,1)} %reshape.185) | copy-start | bytes 1572868
  107.0 3.6 %copy-start.3 = (bf16[128,4,4,128]{3,2,1,0:T(4,128)(2,1)S(1)}, bf16[128,4,4,128]{3,2,1,0:T(4,128)(2,1)}, u32[]{:S(2)}) copy-start(bf16[128,4,4,128]{3,2,1,0:T(4,128)(2,1)} %reshape.183) | copy-start | bytes 1572868
  109.4 1.2 copy-start
  110.6 1.5 copy-start.8
  113.5 27.8 %copy-start.1 = (bf16[4,4,128,384]{2,3,1,0:T(8,128)(2,1)S(1)}, bf16[4,4,128,384]{2,3,1,0:T(8,128)(2,1)}, u32[]{:S(2)}) copy-start(bf16[4,4,128,384]{2,3,1,0:T(8,128)(2,1)} %copy-done) | copy-start | bytes 4718596
  118.2 40.6 %collective-permute-start.3 = (f32[2,128,512]{2,1,0:T(8,128)}, f32[2,128,512]{2,1,0:T(8,128)}, u32[]{:S(2)}, u32[]{:S(2)}) collective-permute-start(f32[2,128,512]{2,1,0:T(8,128)} %get-tuple-element.112), channel_id=1, source_target_pairs={{2,0},{3,1},{4,2},{5,3},{6,4},{7,5},{8,6},{9,7},{10,8},{11,9},{12,... | collective-permute-start | bytes 1572872 | tf_op jit(solution)/shard_map/ppermute | solution.py:15
  135.9 32.0 %collective-permute-start.2 = (f32[2,128,512]{2,1,0:T(8,128)}, f32[2,128,512]{2,1,0:T(8,128)}, u32[]{:S(2)}, u32[]{:S(2)}) collective-permute-start(f32[2,128,512]{2,1,0:T(8,128)} %get-tuple-element.111), channel_id=1, source_target_pairs={{1,0},{2,1},{3,2},{4,3},{5,4},{6,5},{7,6},{8,7},{9,8},{10,9},{11,1... | collective-permute-start | bytes 1572872 | tf_op jit(solution)/shard_map/ppermute | solution.py:15
where the time goes:
time: 173 us; the launch traced here: 171 us
  local copies, waits for them, and re-layouts  47.5 us (27%)
  starting transfers between devices  29.5 us (17%)
  blocking collectives  27.4 us (16%)
  waiting for transfers between devices  23.3 us (13%)
  loops' own time  21.7 us (13%)
  matrix products  9.68 us (6%)
  other arithmetic  9.26 us (5%)
  between operations  2.24 us (1%)
    ppermute x4, starting transfers between devices, passed_along(): return lax.ppermute(array, axis, pairs)  29.5 us
    unnamed x2, blocking collectives  27.4 us
    ppermute x4, waiting for transfers between devices, passed_along(): return lax.ppermute(array, axis, pairs)  23.3 us
    another operation x1, loops' own time, entering(): return lax.fori_loop(0, count, lap, start)  21.7 us
    dynamic_slice x32, local copies, waits for them, and re-layouts, lap(): new = combine(before, everything[k])  18.8 us
    unnamed x32, local copies, waits for them, and re-layouts  14.9 us
    another operation x3, local copies, waits for them, and re-layouts, on_device(): jnp.stack([summand_keys, summand_values])  3.96 us
  transfers between devices with their start and end apart: 4, of which 2 were waited for; matrix products, arithmetic and copies ran while one was open for 23% of the time, Pallas kernels for 0%

commit v1 on v0

v1 whole, which is shorter than its diff:
```python
import jax
import jax.numpy as jnp
from jax import lax
from jax.experimental import pallas as pl
from jax.experimental.pallas import tpu as pltpu
from jax.sharding import PartitionSpec as P

KV_HEADS = 4
GROUP = 4
D = 128
ROWS = 128
WIDE = GROUP * D
SCALE = D**-0.5
LOG2E = 1.4426950408889634
NEG = -1e30
X = 4
Y = 4
DP = 32
CTX = 32
MESH = pl.DeviceIdType.MESH


def dot(a, b, contract):
    return lax.dot_general(
        a, b, ((contract[:1], contract[1:]), ((), ())), preferred_element_type=jnp.float32
    )


def stacked(ref, h):
    return jnp.concatenate(
        [ref[:, h * WIDE + g * D : h * WIDE + (g + 1) * D] for g in range(GROUP)], axis=0
    )


def body(
    q_hbm, k_hbm, v_hbm, g_hbm, size_hbm, pad_hbm,
    o_hbm, dq_hbm, dk_hbm, dv_hbm,
    q, g, kv, size_row, pad_row, meta,
    t2, r2, u, ru, t1, t0, o, dq, dkv,
    in_sem, out_sem, f_send, f_recv, b_send, b_recv, m_send, m_recv,
):
    dp, ctx = lax.axis_index("dp"), lax.axis_index("ctx")
    block = dp * CTX + ctx
    after = lax.rem(block + 1, DP * CTX)
    ahead = (after // CTX, lax.rem(after, CTX))
    before = lax.rem(block + DP * CTX - 1, DP * CTX)
    behind = (before // CTX, lax.rem(before, CTX))
    core = lax.rem(dp, 2)
    x = lax.rem(dp // 2, X)
    y = dp // (2 * X)
    pair = (dp + 1 - 2 * core, ctx)
    along_x = [((y * X + lax.rem(x + j, X)) * 2 + core, ctx) for j in range(1, X)]
    along_y = [((lax.rem(y + j, Y) * X + x) * 2 + core, ctx) for j in range(1, Y)]

    tiny = [
        pltpu.make_async_copy(size_hbm, size_row, in_sem.at[0]),
        pltpu.make_async_copy(pad_hbm, pad_row, in_sem.at[1]),
    ]
    loads = []
    for h in range(KV_HEADS):
        cols = pl.ds(h * D, D)
        wide = pl.ds(h * WIDE, WIDE)
        loads.append([
            pltpu.make_async_copy(q_hbm.at[:, wide], q.at[:, wide], in_sem.at[2 + h * 4]),
            pltpu.make_async_copy(g_hbm.at[:, wide], g.at[:, wide], in_sem.at[3 + h * 4]),
            pltpu.make_async_copy(
                k_hbm.at[:, cols], kv.at[0, h, pl.ds(2 * ROWS, ROWS)], in_sem.at[4 + h * 4]),
            pltpu.make_async_copy(
                v_hbm.at[:, cols], kv.at[1, h, pl.ds(2 * ROWS, ROWS)], in_sem.at[5 + h * 4]),
        ])
    for c in tiny:
        c.start()

    barrier = pltpu.get_barrier_semaphore()
    peers = [ahead, behind, pair] + along_x + along_y
    for peer in peers:
        pl.semaphore_signal(barrier, inc=1, device_id=peer, device_id_type=MESH)
    for group in loads:
        for c in group:
            c.start()
    meta[pl.ds(dp, 1)] = jnp.zeros((1, 2, 128), jnp.int32)
    for c in tiny:
        c.wait()
    meta[pl.ds(dp, 1), 0:1, 0:16] = size_row[...].reshape(1, 1, 16)
    meta[pl.ds(dp, 1), 1:2, 0:16] = pad_row[...].reshape(1, 1, 16)
    pl.semaphore_wait(barrier, len(peers))

    def own_send(h):
        return [
            pltpu.make_async_remote_copy(
                src_ref=(k_hbm, v_hbm)[i].at[:, pl.ds(h * D, D)],
                dst_ref=kv.at[i, h, pl.ds(ROWS, ROWS)],
                send_sem=f_send.at[0, h, i], recv_sem=f_recv.at[0, h, i],
                device_id=ahead, device_id_type=MESH)
            for i in range(2)
        ]

    def relay_send(h):
        return [
            pltpu.make_async_remote_copy(
                src_ref=kv.at[i, h, pl.ds(ROWS, ROWS)],
                dst_ref=kv.at[i, h, pl.ds(0, ROWS)],
                send_sem=f_send.at[1, h, i], recv_sem=f_recv.at[1, h, i],
                device_id=ahead, device_id_type=MESH)
            for i in range(2)
        ]

    def back_send(stage, h, i):
        return pltpu.make_async_remote_copy(
            src_ref=(t2, u)[stage].at[i, h], dst_ref=(r2, ru)[stage].at[i, h],
            send_sem=b_send.at[stage, h, i], recv_sem=b_recv.at[stage, h, i],
            device_id=behind, device_id_type=MESH)

    def meta_send(first, count, device, slot):
        rows = meta.at[pl.ds(first, count)]
        return pltpu.make_async_remote_copy(
            src_ref=rows, dst_ref=rows, send_sem=m_send.at[slot], recv_sem=m_recv.at[slot],
            device_id=device, device_id_type=MESH)

    def landing(first, count, slot):
        rows = meta.at[pl.ds(first, count)]
        return pltpu.make_async_remote_copy(
            src_ref=rows, dst_ref=rows, send_sem=m_send.at[slot], recv_sem=m_recv.at[slot],
            device_id=pair, device_id_type=MESH)

    own = [own_send(h) for h in range(KV_HEADS)]
    relay = [relay_send(h) for h in range(KV_HEADS)]

    def start(copies):
        for c in copies:
            c.start()

    def relay_on(h):
        for a, b in zip(own[h], relay[h]):
            a.wait_recv()
            b.start()

    m1 = meta_send(dp, 1, pair, 0)
    m1.start()
    start(own[0])
    start(own[1])
    landing(dp + 1 - 2 * core, 1, 0).wait_recv()
    m2 = [meta_send(dp - core, 2, along_x[j - 1], j) for j in range(1, X)]
    start(m2)
    relay_on(0)
    start(own[2])
    for j in range(1, X):
        landing((y * X + lax.rem(x + X - j, X)) * 2, 2, j).wait_recv()
    m3 = [meta_send(y * X * 2, 2 * X, along_y[j - 1], X - 1 + j) for j in range(1, Y)]
    start(m3)
    relay_on(1)
    start(own[3])
    for j in range(1, Y):
        landing(lax.rem(y + Y - j, Y) * X * 2, 2 * X, X - 1 + j).wait_recv()

    sizes = meta[:, 0, :].astype(jnp.float32)
    pads = meta[:, 1, :].astype(jnp.float32)
    sizes16 = sizes.astype(jnp.bfloat16)
    below = (
        lax.broadcasted_iota(jnp.int32, (128, 128), 0)
        < lax.broadcasted_iota(jnp.int32, (128, 128), 1)
    )
    inside = dot(sizes16, jnp.where(below, 1.0, 0.0).astype(jnp.bfloat16), (1, 0))
    totals = dot(sizes16, jnp.ones((128, 128), jnp.bfloat16), (1, 0))
    over = (
        lax.broadcasted_iota(jnp.int32, (DP, DP), 1)
        < lax.broadcasted_iota(jnp.int32, (DP, DP), 0)
    )
    lead = dot(
        jnp.where(over, 1.0, 0.0).astype(jnp.bfloat16), totals.astype(jnp.bfloat16), (1, 0)
    )
    offset = block.astype(jnp.float32) - (inside + lead)
    mine = (offset >= 0.0) & (offset < sizes)

    def total(a):
        return jnp.sum(jnp.sum(a, axis=0, keepdims=True), axis=1, keepdims=True)

    place = total(jnp.where(mine, offset, 0.0))
    valid = total(
        jnp.where(mine, jnp.minimum((sizes - offset) * float(ROWS) - pads, float(ROWS)), 0.0)
    )
    bias2 = jnp.where(place >= 1.5, 0.0, NEG)
    bias1 = jnp.where(place >= 0.5, 0.0, NEG)
    slot = lax.broadcasted_iota(jnp.int32, (1, ROWS), 1).astype(jnp.float32)
    live1 = jnp.where(slot < valid, 1.0, 0.0)
    live = jnp.concatenate([live1] * GROUP, axis=1)
    tri1 = jnp.where(
        lax.broadcasted_iota(jnp.int32, (ROWS, ROWS), 0)
        <= lax.broadcasted_iota(jnp.int32, (ROWS, ROWS), 1),
        0.0, NEG,
    )
    tri = jnp.concatenate([tri1] * GROUP, axis=1)

    stores = []

    def store(src, dst, n):
        c = pltpu.make_async_copy(src, dst, out_sem.at[n])
        c.start()
        stores.append(c)

    back = {}

    def head(h):
        wide = pl.ds(h * WIDE, WIDE)
        for c in loads[h]:
            c.wait()
        qs, gs = stacked(q, h), stacked(g, h)
        for c in relay[h]:
            c.wait_recv()
        keys, vals = kv[0, h], kv[1, h]
        s = dot(keys, qs, (1, 1)) * (SCALE * LOG2E)
        s = jnp.concatenate(
            [s[:ROWS] + bias2, s[ROWS : 2 * ROWS] + bias1, s[2 * ROWS :] + tri], axis=0
        )
        e = jnp.exp2(s - jnp.max(s, axis=0, keepdims=True))
        p = e * (live / jnp.sum(e, axis=0, keepdims=True))
        p16 = p.astype(jnp.bfloat16)
        dval = dot(p16, gs, (1, 0))
        t2[1, h] = dval[:ROWS].astype(jnp.bfloat16)
        back[0, h, 1] = back_send(0, h, 1)
        back[0, h, 1].start()
        t1[1, h] = dval[ROWS : 2 * ROWS]
        t0[1, h] = dval[2 * ROWS :]
        dp_ = dot(vals, gs, (1, 1))
        delta = jnp.sum(p * dp_, axis=0, keepdims=True)
        ds = (p * (dp_ - delta)).astype(jnp.bfloat16)
        dkey = dot(ds, qs, (1, 0))
        t2[0, h] = dkey[:ROWS].astype(jnp.bfloat16)
        back[0, h, 0] = back_send(0, h, 0)
        back[0, h, 0].start()
        t1[0, h] = dkey[ROWS : 2 * ROWS]
        t0[0, h] = dkey[2 * ROWS :]
        ot = dot(vals, p16, (0, 0))
        qt = dot(keys, ds, (0, 0)) * SCALE
        for i in range(GROUP):
            at = slice(h * WIDE + i * D, h * WIDE + (i + 1) * D)
            o[:, at] = ot[:, i * D : (i + 1) * D].T.astype(jnp.bfloat16)
            dq[:, at] = qt[:, i * D : (i + 1) * D].T.astype(jnp.bfloat16)
        store(o.at[:, wide], o_hbm.at[:, wide], h * 2)
        store(dq.at[:, wide], dq_hbm.at[:, wide], h * 2 + 1)

    def middle(h):
        for i in (1, 0):
            back[0, h, i].wait_recv()
            u[i, h] = (t1[i, h] + r2[i, h].astype(jnp.float32)).astype(jnp.bfloat16)
            back[1, h, i] = back_send(1, h, i)
            back[1, h, i].start()

    def last(h):
        cols = pl.ds(h * D, D)
        for i in (1, 0):
            back[1, h, i].wait_recv()
            full = t0[i, h] + ru[i, h].astype(jnp.float32)
            if i == 0:
                full = full * SCALE
            dkv[i, :, cols] = full.astype(jnp.bfloat16)
            store(dkv.at[i, :, cols], (dk_hbm, dv_hbm)[i].at[:, cols], 8 + h * 2 + i)

    head(0)
    relay_on(2)
    relay_on(3)
    head(1)
    middle(0)
    head(2)
    middle(1)
    last(0)
    head(3)
    middle(2)
    last(1)
    middle(3)
    last(2)
    last(3)

    for h in range(KV_HEADS):
        for c in own[h] + relay[h]:
            c.wait_send()
        for stage in range(2):
            for i in range(2):
                back[stage, h, i].wait_send()
    for c in [m1] + m2 + m3:
        c.wait_send()
    for c in stores:
        c.wait()


def on_device(queries, keys, values, output_gradient, doc_blocks, doc_pad):
    hbm = pl.BlockSpec(memory_space=pltpu.HBM)
    bf16, f32 = jnp.bfloat16, jnp.float32
    terms = (2, KV_HEADS, ROWS, D)
    return pl.pallas_call(
        body,
        out_shape=(
            jax.ShapeDtypeStruct(queries.shape, bf16),
            jax.ShapeDtypeStruct(queries.shape, bf16),
            jax.ShapeDtypeStruct(keys.shape, bf16),
            jax.ShapeDtypeStruct(keys.shape, bf16),
        ),
        in_specs=[hbm] * 6,
        out_specs=(pl.BlockSpec(memory_space=pl.ANY),) * 4,
        scratch_shapes=[
            pltpu.VMEM(queries.shape, bf16),
            pltpu.VMEM(queries.shape, bf16),
            pltpu.VMEM((2, KV_HEADS, 3 * ROWS, D), bf16),
            pltpu.VMEM((1, 16), jnp.int32),
            pltpu.VMEM((1, 16), jnp.int32),
            pltpu.VMEM((DP, 2, 128), jnp.int32),
            pltpu.VMEM(terms, bf16),
            pltpu.VMEM(terms, bf16),
            pltpu.VMEM(terms, bf16),
            pltpu.VMEM(terms, bf16),
            pltpu.VMEM(terms, f32),
            pltpu.VMEM(terms, f32),
            pltpu.VMEM(queries.shape, bf16),
            pltpu.VMEM(queries.shape, bf16),
            pltpu.VMEM((2, ROWS, KV_HEADS * D), bf16),
            pltpu.SemaphoreType.DMA((18,)),
            pltpu.SemaphoreType.DMA((16,)),
            pltpu.SemaphoreType.DMA((2, KV_HEADS, 2)),
            pltpu.SemaphoreType.DMA((2, KV_HEADS, 2)),
            pltpu.SemaphoreType.DMA((2, KV_HEADS, 2)),
            pltpu.SemaphoreType.DMA((2, KV_HEADS, 2)),
            pltpu.SemaphoreType.DMA((X + Y - 1,)),
            pltpu.SemaphoreType.DMA((X + Y - 1,)),
        ],
        compiler_params=pltpu.CompilerParams(
            collective_id=0, has_side_effects=True, vmem_limit_bytes=40 * 1024 * 1024
        ),
    )(*[
        pltpu.with_memory_space_constraint(a, pltpu.HBM)
        for a in (
            queries, keys, values, output_gradient,
            doc_blocks.reshape(1, 16), doc_pad.reshape(1, 16),
        )
    ])


def solution(mesh):
    tokens = P(("dp", "ctx"), None)
    return jax.shard_map(
        on_device,
        mesh=mesh,
        in_specs=(tokens, tokens, tokens, tokens, P("dp"), P("dp")),
        out_specs=(tokens, tokens, tokens, tokens),
        check_vma=False,
    )
```

time: 173 us -> 47.8 us (0.28); the launches traced: 171 us -> 47.4 us
  local copies, waits for them, and re-layouts: 47.5 us -> 2.9 us
  Pallas kernels: 0 us -> 43.9 us
  starting transfers between devices: 29.5 us -> 0 us
  blocking collectives: 27.4 us -> 0 us
  waiting for transfers between devices: 23.3 us -> 0 us
  loops' own time: 21.7 us -> 0 us
  matrix products: 9.68 us -> 0 us
  other arithmetic: 9.26 us -> 0 us
    pallas_call x0 -> x1, Pallas kernels: none -> 43.9 us  [on_device(): pl.pallas_call(body, out_shape=(jax.ShapeDtypeStruct(queries.shape, bf16)...]
    ppermute x4 -> x0, starting transfers between devices: 29.5 us -> none  [passed_along(): return lax.ppermute(array, axis, pairs)]
    unnamed x2 -> x0, blocking collectives: 27.4 us -> none
    ppermute x4 -> x0, waiting for transfers between devices: 23.3 us -> none  [passed_along(): return lax.ppermute(array, axis, pairs)]
    another operation x1 -> x0, loops' own time: 21.7 us -> none  [entering(): return lax.fori_loop(0, count, lap, start)]
    dynamic_slice x32 -> x0, local copies, waits for them, and re-layouts: 18.8 us -> none  [lap(): new = combine(before, everything[k])]
    unnamed x32 -> x4, local copies, waits for them, and re-layouts: 14.9 us -> 2.9 us
    dot_general x6 -> x0, matrix products: 9.68 us -> none  [the longest x1 2.82 us: on_device(): jnp.einsum('kgts,tkgd->skd', weight_bf16, gradient_heads, preferred_eleme...]
  transfers between devices with their start and end apart: 4 -> 0, of which waited for: 2 -> 0; matrix products, arithmetic and copies ran while one was open for 23% -> 0% of each run, Pallas kernels for 0% -> 0%
where the time goes in v1:
time: 47.8 us; the launch traced here: 47.4 us
  Pallas kernels  43.9 us (92%)
  local copies, waits for them, and re-layouts  2.9 us (6%)
  between operations  0.64 us (1%)
    pallas_call x1, Pallas kernels, on_device(): pl.pallas_call(body, out_shape=(jax.ShapeDtypeStruct(queries.shape, bf16)...  43.9 us
    unnamed x4, local copies, waits for them, and re-layouts  2.9 us

profile of v1, /device:TPU:25, one launch (start us, length us, event | category | flops | bytes accessed | tf_op | source)
XLA Modules:
  0.0 47.4 jit_solution(7720744723412877050)
XLA Ops:
  0.6 43.9 %shard_map.93 = (bf16[128,2048]{1,0:T(8,128)(2,1)S(1)}, bf16[128,2048]{1,0:T(8,128)(2,1)S(1)}, bf16[128,512]{1,0:T(8,128)(2,1)S(1)}, bf16[128,512]{1,0:T(8,128)(2,1)S(1)}) custom-call(bf16[128,2048]{1,0:T(8,128)(2,1)} %q_hbm.1, bf16[128,512]{1,0:T(8,128)(2,1)} %k_hbm.1, bf16[128,512]{1,0:T(8,128)(2,1)} %v_hbm.1, bf16[128,2048]{1,0:T(8,128)(2,1)} %g_hbm.1, ...), custom_call_target="tpu_custom_call" | custom-call | tf_op jit(solution)/shard_map/pallas_call | solution.py:290
  44.5 0.8 %copy.14 = bf16[128,2048]{1,0:T(8,128)(2,1)} copy(bf16[128,2048]{1,0:T(8,128)(2,1)S(1)} %get-tuple-element.8) | data formatting | bytes 1048576
  45.3 0.8 %copy.15 = bf16[128,2048]{1,0:T(8,128)(2,1)} copy(bf16[128,2048]{1,0:T(8,128)(2,1)S(1)} %get-tuple-element.9) | data formatting | bytes 1048576
  46.1 0.7 %copy.16 = bf16[128,512]{1,0:T(8,128)(2,1)} copy(bf16[128,512]{1,0:T(8,128)(2,1)S(1)} %get-tuple-element.10) | data formatting | bytes 262144
  46.8 0.7 %copy.17 = bf16[128,512]{1,0:T(8,128)(2,1)} copy(bf16[128,512]{1,0:T(8,128)(2,1)S(1)} %get-tuple-element.11) | data formatting | bytes 262144

commit v2 on v1

v2 whole, which is shorter than its diff:
```python
import jax
import jax.numpy as jnp
from jax import lax
from jax.experimental import pallas as pl
from jax.experimental.pallas import tpu as pltpu
from jax.sharding import PartitionSpec as P

KV_HEADS = 4
GROUP = 4
D = 128
ROWS = 128
WIDE = GROUP * D
SCALE = D**-0.5
LOG2E = 1.4426950408889634
NEG = -1e30
X = 4
Y = 4
DP = 32
CTX = 32
MESH = pl.DeviceIdType.MESH


def dot(a, b, contract):
    return lax.dot_general(
        a, b, ((contract[:1], contract[1:]), ((), ())), preferred_element_type=jnp.float32
    )


def stacked(ref, h):
    return jnp.concatenate(
        [ref[:, h * WIDE + g * D : h * WIDE + (g + 1) * D] for g in range(GROUP)], axis=0
    )


def body(
    q_hbm, k_hbm, v_hbm, g_hbm, size_hbm, pad_hbm,
    o, dq, dk, dv,
    q, g, kv, size_row, pad_row, meta, ex, dpr, stat,
    t2, r2, u, ru, t1, t0,
    in_sem, f_send, f_recv, b_send, b_recv, m_send, m_recv,
):
    dp, ctx = lax.axis_index("dp"), lax.axis_index("ctx")
    block = dp * CTX + ctx
    after = lax.rem(block + 1, DP * CTX)
    ahead = (after // CTX, lax.rem(after, CTX))
    before = lax.rem(block + DP * CTX - 1, DP * CTX)
    behind = (before // CTX, lax.rem(before, CTX))
    core = lax.rem(dp, 2)
    x = lax.rem(dp // 2, X)
    y = dp // (2 * X)
    pair = (dp + 1 - 2 * core, ctx)
    along_x = [((y * X + lax.rem(x + j, X)) * 2 + core, ctx) for j in range(1, X)]
    along_y = [((lax.rem(y + j, Y) * X + x) * 2 + core, ctx) for j in range(1, Y)]

    barrier = pltpu.get_barrier_semaphore()
    peers = [pair] + along_x + along_y
    for peer in [behind] + peers:
        pl.semaphore_signal(barrier, inc=1, device_id=peer, device_id_type=MESH)

    tiny = [
        pltpu.make_async_copy(size_hbm, size_row, in_sem.at[0]),
        pltpu.make_async_copy(pad_hbm, pad_row, in_sem.at[1]),
    ]
    loads = []
    for h in range(KV_HEADS):
        cols = pl.ds(h * D, D)
        wide = pl.ds(h * WIDE, WIDE)
        loads.append([
            pltpu.make_async_copy(
                k_hbm.at[:, cols], kv.at[0, h, pl.ds(2 * ROWS, ROWS)], in_sem.at[4 + h * 4]),
            pltpu.make_async_copy(q_hbm.at[:, wide], q.at[:, wide], in_sem.at[2 + h * 4]),
            pltpu.make_async_copy(
                v_hbm.at[:, cols], kv.at[1, h, pl.ds(2 * ROWS, ROWS)], in_sem.at[5 + h * 4]),
            pltpu.make_async_copy(g_hbm.at[:, wide], g.at[:, wide], in_sem.at[3 + h * 4]),
        ])
    for group in [tiny] + loads:
        for c in group:
            c.start()
    meta[pl.ds(dp, 1)] = jnp.zeros((1, 2, 128), jnp.int32)
    for c in tiny:
        c.wait()
    meta[pl.ds(dp, 1), 0:1, 0:16] = size_row[...].reshape(1, 1, 16)
    meta[pl.ds(dp, 1), 1:2, 0:16] = pad_row[...].reshape(1, 1, 16)
    pl.semaphore_wait(barrier, 1 + len(peers))

    def own_send(h):
        return [
            pltpu.make_async_remote_copy(
                src_ref=(k_hbm, v_hbm)[i].at[:, pl.ds(h * D, D)],
                dst_ref=kv.at[i, h, pl.ds(ROWS, ROWS)],
                send_sem=f_send.at[0, h, i], recv_sem=f_recv.at[0, h, i],
                device_id=ahead, device_id_type=MESH)
            for i in range(2)
        ]

    def relay_send(h):
        return [
            pltpu.make_async_remote_copy(
                src_ref=kv.at[i, h, pl.ds(ROWS, ROWS)],
                dst_ref=kv.at[i, h, pl.ds(0, ROWS)],
                send_sem=f_send.at[1, h, i], recv_sem=f_recv.at[1, h, i],
                device_id=ahead, device_id_type=MESH)
            for i in range(2)
        ]

    def back_send(stage, h, i):
        return pltpu.make_async_remote_copy(
            src_ref=(t2, u)[stage].at[i, h], dst_ref=(r2, ru)[stage].at[i, h],
            send_sem=b_send.at[stage, h, i], recv_sem=b_recv.at[stage, h, i],
            device_id=behind, device_id_type=MESH)

    def meta_send(first, count, device, slot):
        rows = meta.at[pl.ds(first, count)]
        return pltpu.make_async_remote_copy(
            src_ref=rows, dst_ref=rows, send_sem=m_send.at[slot], recv_sem=m_recv.at[slot],
            device_id=device, device_id_type=MESH)

    own = [own_send(h) for h in range(KV_HEADS)]
    relay = [relay_send(h) for h in range(KV_HEADS)]

    def start(copies):
        for c in copies:
            c.start()

    def relay_on(h):
        for a, b in zip(own[h], relay[h]):
            a.wait_recv()
            b.start()

    stacks = {}

    def part(h, at):
        rows = slice((2 - at) * ROWS, (3 - at) * ROWS)
        qs, gs = stacked(q, h), stacked(g, h)
        s = dot(kv[0, h, rows], qs, (1, 1)) * (SCALE * LOG2E)
        if at == 0:
            s = s + jnp.concatenate([tri] * GROUP, axis=1)
        peak = jnp.max(s, axis=0, keepdims=True)
        e = jnp.exp2(s - peak)
        r = dot(kv[1, h, rows], gs, (1, 1))
        ex[h, rows] = e
        dpr[h, rows] = r
        stat[h, at, 0:1] = peak
        stat[h, at, 1:2] = jnp.sum(e, axis=0, keepdims=True)
        stat[h, at, 2:3] = jnp.sum(e * r, axis=0, keepdims=True)

    tri = jnp.where(
        lax.broadcasted_iota(jnp.int32, (ROWS, ROWS), 0)
        <= lax.broadcasted_iota(jnp.int32, (ROWS, ROWS), 1),
        0.0, NEG,
    )

    m1 = meta_send(dp, 1, pair, 0)
    m1.start()
    for h in range(KV_HEADS):
        start(own[h])
    for c in loads[0]:
        c.wait()
    part(0, 0)
    meta_send(dp + 1 - 2 * core, 1, pair, 0).wait_recv()
    m2 = [meta_send(dp - core, 2, along_x[j - 1], j) for j in range(1, X)]
    start(m2)
    for c in loads[1]:
        c.wait()
    part(1, 0)
    for j in range(1, X):
        meta_send((y * X + lax.rem(x + X - j, X)) * 2, 2, pair, j).wait_recv()
    m3 = [meta_send(y * X * 2, 2 * X, along_y[j - 1], X - 1 + j) for j in range(1, Y)]
    start(m3)
    relay_on(0)
    for c in loads[2]:
        c.wait()
    part(2, 0)
    relay_on(1)
    for c in loads[3]:
        c.wait()
    part(3, 0)
    relay_on(2)
    part(0, 1)
    for j in range(1, Y):
        meta_send(lax.rem(y + Y - j, Y) * X * 2, 2 * X, pair, X - 1 + j).wait_recv()
    relay_on(3)

    sizes = meta[:, 0, :].astype(jnp.float32)
    pads = meta[:, 1, :].astype(jnp.float32)
    sizes16 = sizes.astype(jnp.bfloat16)
    below = (
        lax.broadcasted_iota(jnp.int32, (128, 128), 0)
        < lax.broadcasted_iota(jnp.int32, (128, 128), 1)
    )
    inside = dot(sizes16, jnp.where(below, 1.0, 0.0).astype(jnp.bfloat16), (1, 0))
    totals = dot(sizes16, jnp.ones((128, 128), jnp.bfloat16), (1, 0))
    over = (
        lax.broadcasted_iota(jnp.int32, (DP, DP), 1)
        < lax.broadcasted_iota(jnp.int32, (DP, DP), 0)
    )
    lead = dot(
        jnp.where(over, 1.0, 0.0).astype(jnp.bfloat16), totals.astype(jnp.bfloat16), (1, 0)
    )
    offset = block.astype(jnp.float32) - (inside + lead)
    mine = (offset >= 0.0) & (offset < sizes)

    def total(a):
        return jnp.sum(jnp.sum(a, axis=0, keepdims=True), axis=1, keepdims=True)

    place = total(jnp.where(mine, offset, 0.0))
    valid = total(
        jnp.where(mine, jnp.minimum((sizes - offset) * float(ROWS) - pads, float(ROWS)), 0.0)
    )
    bias = [None, jnp.where(place >= 0.5, 0.0, NEG), jnp.where(place >= 1.5, 0.0, NEG)]
    slot = lax.broadcasted_iota(jnp.int32, (1, ROWS), 1).astype(jnp.float32)
    live1 = jnp.where(slot < valid, 1.0, 0.0)
    live = jnp.concatenate([live1] * GROUP, axis=1)

    back = {}

    def send_back(stage, h, i):
        back[stage, h, i] = back_send(stage, h, i)
        back[stage, h, i].start()

    def finish(h):
        qs, gs = stacked(q, h), stacked(g, h)
        peaks = [stat[h, 0, 0:1]] + [stat[h, at, 0:1] + bias[at] for at in (1, 2)]
        top = jnp.maximum(jnp.maximum(peaks[0], peaks[1]), peaks[2])
        w = [jnp.exp2(p - top) for p in peaks]
        whole = sum(w[at] * stat[h, at, 1:2] for at in range(3))
        share = live / whole
        delta = sum(w[at] * stat[h, at, 2:3] for at in range(3)) * share
        p16, ds16 = {}, {}
        for at in (2, 1, 0):
            rows = slice((2 - at) * ROWS, (3 - at) * ROWS)
            p = ex[h, rows] * (w[at] * share)
            p16[at] = p.astype(jnp.bfloat16)
            ds16[at] = (p * (dpr[h, rows] - delta)).astype(jnp.bfloat16)
            dval = dot(p16[at], gs, (1, 0))
            dkey = dot(ds16[at], qs, (1, 0))
            if at == 2:
                t2[1, h] = dval.astype(jnp.bfloat16)
                send_back(0, h, 1)
                t2[0, h] = dkey.astype(jnp.bfloat16)
                send_back(0, h, 0)
            else:
                keep = (t0, t1)[at]
                keep[1, h] = dval
                keep[0, h] = dkey
        stacks[h] = (
            jnp.concatenate([p16[2], p16[1], p16[0]], axis=0),
            jnp.concatenate([ds16[2], ds16[1], ds16[0]], axis=0),
        )

    def outputs(h):
        p16, ds16 = stacks[h]
        ot = dot(kv[1, h], p16, (0, 0))
        qt = dot(kv[0, h], ds16, (0, 0)) * SCALE
        for i in range(GROUP):
            at = slice(h * WIDE + i * D, h * WIDE + (i + 1) * D)
            o[:, at] = ot[:, i * D : (i + 1) * D].T.astype(jnp.bfloat16)
            dq[:, at] = qt[:, i * D : (i + 1) * D].T.astype(jnp.bfloat16)

    def head(h):
        for c in relay[h]:
            c.wait_recv()
        part(h, 2)
        finish(h)
        outputs(h)

    def middle(h):
        for i in (1, 0):
            back[0, h, i].wait_recv()
            u[i, h] = (t1[i, h] + r2[i, h].astype(jnp.float32)).astype(jnp.bfloat16)
            send_back(1, h, i)

    def last(h):
        cols = slice(h * D, (h + 1) * D)
        for i in (1, 0):
            back[1, h, i].wait_recv()
            full = t0[i, h] + ru[i, h].astype(jnp.float32)
            if i == 0:
                dk[:, cols] = (full * SCALE).astype(jnp.bfloat16)
            else:
                dv[:, cols] = full.astype(jnp.bfloat16)

    part(1, 1)
    part(2, 1)
    part(3, 1)
    head(0)
    head(1)
    middle(0)
    head(2)
    middle(1)
    last(0)
    head(3)
    middle(2)
    last(1)
    middle(3)
    last(2)
    last(3)

    for h in range(KV_HEADS):
        for c in own[h] + relay[h]:
            c.wait_send()
        for stage in range(2):
            for i in range(2):
                back[stage, h, i].wait_send()
    for c in [m1] + m2 + m3:
        c.wait_send()


def write_out(*refs):
    sources, targets, sem = refs[:4], refs[4:8], refs[8]
    copies = [
        pltpu.make_async_copy(a, b, sem.at[i])
        for i, (a, b) in enumerate(zip(sources, targets))
    ]
    for c in copies:
        c.start()
    for c in copies:
        c.wait()


def on_device(queries, keys, values, output_gradient, doc_blocks, doc_pad):
    hbm = pl.BlockSpec(memory_space=pltpu.HBM)
    anywhere = pl.BlockSpec(memory_space=pl.ANY)
    bf16, f32 = jnp.bfloat16, jnp.float32
    terms = (2, KV_HEADS, ROWS, D)
    scores = (KV_HEADS, 3 * ROWS, WIDE)
    shapes = (queries.shape, queries.shape, keys.shape, keys.shape)
    results = pl.pallas_call(
        body,
        out_shape=tuple(jax.ShapeDtypeStruct(shape, bf16) for shape in shapes),
        in_specs=[hbm] * 6,
        out_specs=(pl.BlockSpec(memory_space=pltpu.VMEM),) * 4,
        scratch_shapes=[
            pltpu.VMEM(queries.shape, bf16),
            pltpu.VMEM(queries.shape, bf16),
            pltpu.VMEM((2, KV_HEADS, 3 * ROWS, D), bf16),
            pltpu.VMEM((1, 16), jnp.int32),
            pltpu.VMEM((1, 16), jnp.int32),
            pltpu.VMEM((DP, 2, 128), jnp.int32),
            pltpu.VMEM(scores, f32),
            pltpu.VMEM(scores, f32),
            pltpu.VMEM((KV_HEADS, 3, 8, WIDE), f32),
            pltpu.VMEM(terms, bf16),
            pltpu.VMEM(terms, bf16),
            pltpu.VMEM(terms, bf16),
            pltpu.VMEM(terms, bf16),
            pltpu.VMEM(terms, f32),
            pltpu.VMEM(terms, f32),
            pltpu.SemaphoreType.DMA((18,)),
            pltpu.SemaphoreType.DMA((2, KV_HEADS, 2)),
            pltpu.SemaphoreType.DMA((2, KV_HEADS, 2)),
            pltpu.SemaphoreType.DMA((2, KV_HEADS, 2)),
            pltpu.SemaphoreType.DMA((2, KV_HEADS, 2)),
            pltpu.SemaphoreType.DMA((X + Y - 1,)),
            pltpu.SemaphoreType.DMA((X + Y - 1,)),
        ],
        compiler_params=pltpu.CompilerParams(
            collective_id=0, has_side_effects=True, vmem_limit_bytes=40 * 1024 * 1024
        ),
    )(*[
        pltpu.with_memory_space_constraint(a, pltpu.HBM)
        for a in (
            queries, keys, values, output_gradient,
            doc_blocks.reshape(1, 16), doc_pad.reshape(1, 16),
        )
    ])
    return pl.pallas_call(
        write_out,
        out_shape=tuple(jax.ShapeDtypeStruct(shape, bf16) for shape in shapes),
        in_specs=[pl.BlockSpec(memory_space=pltpu.VMEM)] * 4,
        out_specs=(anywhere,) * 4,
        scratch_shapes=[pltpu.SemaphoreType.DMA((4,))],
    )(*[pltpu.with_memory_space_constraint(a, pltpu.VMEM) for a in results])


def solution(mesh):
    tokens = P(("dp", "ctx"), None)
    return jax.shard_map(
        on_device,
        mesh=mesh,
        in_specs=(tokens, tokens, tokens, tokens, P("dp"), P("dp")),
        out_specs=(tokens, tokens, tokens, tokens),
        check_vma=False,
    )
```

time: 47.8 us -> 44.3 us (0.927)
  local copies, waits for them, and re-layouts: 2.9 us -> 0 us
  Pallas kernels: 43.9 us -> 43.1 us
    unnamed x4 -> x0, local copies, waits for them, and re-layouts: 2.9 us -> none
    pallas_call x1 -> x2, Pallas kernels: 43.9 us -> 43.1 us  [the longest x1 42.1 us: on_device(): pl.pallas_call(body, out_shape=tuple((jax.ShapeDtypeStruct(shape, bf16) f...]
where the time goes in v2:
time: 44.3 us; the launch traced here: 43.8 us
  Pallas kernels  43.1 us (97%)
  between operations  0.64 us (1%)
    pallas_call x1, Pallas kernels, on_device(): pl.pallas_call(body, out_shape=tuple((jax.ShapeDtypeStruct(shape, bf16) f...  42.1 us
    pallas_call x1, Pallas kernels, on_device(): pl.pallas_call(write_out, out_shape=tuple((jax.ShapeDtypeStruct(shape, bf...  1.08 us

profile of v2, /device:TPU:25, one launch (start us, length us, event | category | flops | bytes accessed | tf_op | source)
XLA Modules:
  0.0 43.8 jit_solution(17811232593143857961)
XLA Ops:
  0.6 42.1 %shard_map.93 = (bf16[128,2048]{1,0:T(8,128)(2,1)S(1)}, bf16[128,2048]{1,0:T(8,128)(2,1)S(1)}, bf16[128,512]{1,0:T(8,128)(2,1)S(1)}, bf16[128,512]{1,0:T(8,128)(2,1)S(1)}) custom-call(bf16[128,2048]{1,0:T(8,128)(2,1)} %q_hbm.1, bf16[128,512]{1,0:T(8,128)(2,1)} %k_hbm.1, bf16[128,512]{1,0:T(8,128)(2,1)} %v_hbm.1, bf16[128,2048]{1,0:T(8,128)(2,1)} %g_hbm.1, ...), custom_call_target="tpu_custom_call" | custom-call | tf_op jit(solution)/shard_map/pallas_call | solution.py:328
  42.7 1.1 %shard_map.94 = (bf16[128,2048]{1,0:T(8,128)(2,1)}, bf16[128,2048]{1,0:T(8,128)(2,1)}, bf16[128,512]{1,0:T(8,128)(2,1)}, bf16[128,512]{1,0:T(8,128)(2,1)}) custom-call(bf16[128,2048]{1,0:T(8,128)(2,1)S(1)} %get-tuple-element.8.refs_0_, bf16[128,2048]{1,0:T(8,128)(2,1)S(1)} %get-tuple-element.9.refs_1_, bf16[128,512]{1,0:T(8,128)(2,1)S(1)} %get-tuple-element.10.refs_2_, ...), custom_call_target="tpu_custom_call" | custom-call | tf_op jit(solution)/shard_map/pallas_call | solution.py:367

commit v3 on v2

--- a/solution.py
+++ b/solution.py
@@ -54,8 +54,15 @@
 
     barrier = pltpu.get_barrier_semaphore()
     peers = [pair] + along_x + along_y
-    for peer in [behind] + peers:
-        pl.semaphore_signal(barrier, inc=1, device_id=peer, device_id_type=MESH)
+    in_plane = (ctx > 0) & (ctx < CTX - 2)
+    told = jnp.logical_not(in_plane)
+    pl.semaphore_signal(barrier, inc=1, device_id=behind, device_id_type=MESH)
+
+    @pl.when(in_plane)
+    def _():
+        for peer in peers:
+            pl.semaphore_signal(barrier, inc=1, device_id=peer, device_id_type=MESH)
+
 
     tiny = [
         pltpu.make_async_copy(size_hbm, size_row, in_sem.at[0]),
@@ -73,20 +80,39 @@
                 v_hbm.at[:, cols], kv.at[1, h, pl.ds(2 * ROWS, ROWS)], in_sem.at[5 + h * 4]),
             pltpu.make_async_copy(g_hbm.at[:, wide], g.at[:, wide], in_sem.at[3 + h * 4]),
         ])
-    for group in [tiny] + loads:
-        for c in group:
-            c.start()
-    meta[pl.ds(dp, 1)] = jnp.zeros((1, 2, 128), jnp.int32)
+    for group in loads:
+        group[0].start()
+        group[2].start()
+    for c in tiny:
+        c.start()
+    for group in loads:
+        group[1].start()
+        group[3].start()
     for c in tiny:
         c.wait()
-    meta[pl.ds(dp, 1), 0:1, 0:16] = size_row[...].reshape(1, 1, 16)
-    meta[pl.ds(dp, 1), 1:2, 0:16] = pad_row[...].reshape(1, 1, 16)
-    pl.semaphore_wait(barrier, 1 + len(peers))
+
+    @pl.when(in_plane)
+    def _():
+        meta[pl.ds(dp, 1)] = jnp.zeros((1, 2, 128), jnp.int32)
+        meta[pl.ds(dp, 1), 0:1, 0:16] = size_row[...].reshape(1, 1, 16)
+        meta[pl.ds(dp, 1), 1:2, 0:16] = pad_row[...].reshape(1, 1, 16)
+
+    for group in loads:
+        group[0].wait()
+        group[2].wait()
+
+    @pl.when(told)
+    def _():
+        pl.semaphore_wait(barrier, 1)
+
+    @pl.when(in_plane)
+    def _():
+        pl.semaphore_wait(barrier, 1 + len(peers))
 
     def own_send(h):
         return [
             pltpu.make_async_remote_copy(
-                src_ref=(k_hbm, v_hbm)[i].at[:, pl.ds(h * D, D)],
+                src_ref=kv.at[i, h, pl.ds(2 * ROWS, ROWS)],
                 dst_ref=kv.at[i, h, pl.ds(ROWS, ROWS)],
                 send_sem=f_send.at[0, h, i], recv_sem=f_recv.at[0, h, i],
                 device_id=ahead, device_id_type=MESH)
@@ -151,35 +177,74 @@
     )
 
     m1 = meta_send(dp, 1, pair, 0)
-    m1.start()
-    for h in range(KV_HEADS):
-        start(own[h])
-    for c in loads[0]:
-        c.wait()
+    m2 = [meta_send(dp - core, 2, along_x[j - 1], j) for j in range(1, X)]
+    m3 = [meta_send(y * X * 2, 2 * X, along_y[j - 1], X - 1 + j) for j in range(1, Y)]
+    table = pltpu.make_async_remote_copy(
+        src_ref=meta, dst_ref=meta, send_sem=m_send.at[X + Y - 1], recv_sem=m_recv.at[X + Y - 1],
+        device_id=behind, device_id_type=MESH)
+
+    def exchange_x():
+        @pl.when(in_plane)
+        def _():
+            meta_send(dp + 1 - 2 * core, 1, pair, 0).wait_recv()
+            start(m2)
+
+    def exchange_y():
+        @pl.when(in_plane)
+        def _():
+            for j in range(1, X):
+                meta_send((y * X + lax.rem(x + X - j, X)) * 2, 2, pair, j).wait_recv()
+            start(m3)
+
+    def exchanged():
+        @pl.when(in_plane)
+        def _():
+            for j in range(1, Y):
+                meta_send(lax.rem(y + Y - j, Y) * X * 2, 2 * X, pair, X - 1 + j).wait_recv()
+
+    def wait_rest(h):
+        loads[h][1].wait()
+        loads[h][3].wait()
+
+    pl.when(in_plane)(m1.start)
+    def sent(h):
+        for c in own[h]:
+            c.wait_send()
+
+    start(own[0])
+    start(own[1])
+    wait_rest(0)
     part(0, 0)
-    meta_send(dp + 1 - 2 * core, 1, pair, 0).wait_recv()
-    m2 = [meta_send(dp - core, 2, along_x[j - 1], j) for j in range(1, X)]
-    start(m2)
-    for c in loads[1]:
-        c.wait()
+    sent(0)
+    start(own[2])
+    exchange_x()
+    wait_rest(1)
     part(1, 0)
-    for j in range(1, X):
-        meta_send((y * X + lax.rem(x + X - j, X)) * 2, 2, pair, j).wait_recv()
-    m3 = [meta_send(y * X * 2, 2 * X, along_y[j - 1], X - 1 + j) for j in range(1, Y)]
-    start(m3)
+    exchange_y()
+    wait_rest(2)
+    part(2, 0)
+    sent(1)
+    wait_rest(3)
+    part(3, 0)
+    start(own[3])
     relay_on(0)
-    for c in loads[2]:
-        c.wait()
-    part(2, 0)
+
+    @pl.when(ctx == 0)
+    def _():
+        table.wait_recv()
+        table.start()
+
     relay_on(1)
-    for c in loads[3]:
-        c.wait()
-    part(3, 0)
+    part(0, 1)
     relay_on(2)
-    part(0, 1)
-    for j in range(1, Y):
-        meta_send(lax.rem(y + Y - j, Y) * X * 2, 2 * X, pair, X - 1 + j).wait_recv()
+    part(1, 1)
+    exchanged()
     relay_on(3)
+    pl.when(ctx == 1)(table.start)
+    part(2, 1)
+    part(3, 1)
+    pl.when(ctx >= CTX - 2)(table.wait_recv)
+    pl.when(ctx == CTX - 1)(table.start)
 
     sizes = meta[:, 0, :].astype(jnp.float32)
     pads = meta[:, 1, :].astype(jnp.float32)
@@ -212,11 +277,8 @@
     live1 = jnp.where(slot < valid, 1.0, 0.0)
     live = jnp.concatenate([live1] * GROUP, axis=1)
 
-    back = {}
-
     def send_back(stage, h, i):
-        back[stage, h, i] = back_send(stage, h, i)
-        back[stage, h, i].start()
+        back_send(stage, h, i).start()
 
     def finish(h):
         qs, gs = stacked(q, h), stacked(g, h)
@@ -266,44 +328,53 @@
 
     def middle(h):
         for i in (1, 0):
-            back[0, h, i].wait_recv()
+            back_send(0, h, i).wait_recv()
             u[i, h] = (t1[i, h] + r2[i, h].astype(jnp.float32)).astype(jnp.bfloat16)
             send_back(1, h, i)
 
     def last(h):
         cols = slice(h * D, (h + 1) * D)
         for i in (1, 0):
-            back[1, h, i].wait_recv()
+            back_send(1, h, i).wait_recv()
             full = t0[i, h] + ru[i, h].astype(jnp.float32)
             if i == 0:
                 dk[:, cols] = (full * SCALE).astype(jnp.bfloat16)
             else:
                 dv[:, cols] = full.astype(jnp.bfloat16)
 
-    part(1, 1)
-    part(2, 1)
-    part(3, 1)
-    head(0)
-    head(1)
-    middle(0)
-    head(2)
-    middle(1)
-    last(0)
-    head(3)
-    middle(2)
-    last(1)
-    middle(3)
-    last(2)
-    last(3)
-
+    second = ctx == 1
+
+    def middle_if(h, when):
+        pl.when(when)(lambda: middle(h))
+
+    first = ctx == 0
+    usual = ctx > 1
     for h in range(KV_HEADS):
-        for c in own[h] + relay[h]:
+        head(h)
+        middle_if(h, second)
+        if h >= 1:
+            middle_if(h - 1, first)
+        if h == 2:
+            middle_if(0, usual)
+    middle_if(1, usual)
+    middle_if(2, usual)
+    middle_if(3, jnp.logical_not(second))
+    for h in range(KV_HEADS):
+        last(h)
+
+    for h in range(KV_HEADS):
+        for c in (own[h] if h > 1 else []) + relay[h]:
             c.wait_send()
         for stage in range(2):
             for i in range(2):
-                back[stage, h, i].wait_send()
-    for c in [m1] + m2 + m3:
-        c.wait_send()
+                back_send(stage, h, i).wait_send()
+
+    @pl.when(in_plane)
+    def _():
+        for c in [m1] + m2 + m3:
+            c.wait_send()
+
+    pl.when((ctx <= 1) | (ctx == CTX - 1))(table.wait_send)
 
 
 def write_out(*refs):
@@ -351,8 +422,8 @@
             pltpu.SemaphoreType.DMA((2, KV_HEADS, 2)),
             pltpu.SemaphoreType.DMA((2, KV_HEADS, 2)),
             pltpu.SemaphoreType.DMA((2, KV_HEADS, 2)),
-            pltpu.SemaphoreType.DMA((X + Y - 1,)),
-            pltpu.SemaphoreType.DMA((X + Y - 1,)),
+            pltpu.SemaphoreType.DMA((X + Y,)),
+            pltpu.SemaphoreType.DMA((X + Y,)),
         ],
         compiler_params=pltpu.CompilerParams(
             collective_id=0, has_side_effects=True, vmem_limit_bytes=40 * 1024 * 1024

time: 44.3 us -> 42.5 us (0.959)
  Pallas kernels: 43.1 us -> 41.3 us
    pallas_call x1, Pallas kernels: 42.1 us -> 40.2 us  [on_device(): pl.pallas_call(body, out_shape=tuple((jax.ShapeDtypeStruct(shape, bf16) f...]
where the time goes in v3:
time: 42.5 us; the launch traced here: 41.9 us
  Pallas kernels  41.3 us (97%)
  between operations  0.64 us (2%)
    pallas_call x1, Pallas kernels, on_device(): pl.pallas_call(body, out_shape=tuple((jax.ShapeDtypeStruct(shape, bf16) f...  40.2 us
    pallas_call x1, Pallas kernels, on_device(): pl.pallas_call(write_out, out_shape=tuple((jax.ShapeDtypeStruct(shape, bf...  1.08 us

profile of v3, /device:TPU:25, one launch (start us, length us, event | category | flops | bytes accessed | tf_op | source)
XLA Modules:
  0.0 41.9 jit_solution(15310295572667350564)
XLA Ops:
  0.6 40.2 %shard_map.93 = (bf16[128,2048]{1,0:T(8,128)(2,1)S(1)}, bf16[128,2048]{1,0:T(8,128)(2,1)S(1)}, bf16[128,512]{1,0:T(8,128)(2,1)S(1)}, bf16[128,512]{1,0:T(8,128)(2,1)S(1)}) custom-call(bf16[128,2048]{1,0:T(8,128)(2,1)} %q_hbm.1, bf16[128,512]{1,0:T(8,128)(2,1)} %k_hbm.1, bf16[128,512]{1,0:T(8,128)(2,1)} %v_hbm.1, bf16[128,2048]{1,0:T(8,128)(2,1)} %g_hbm.1, ...), custom_call_target="tpu_custom_call" | custom-call | tf_op jit(solution)/shard_map/pallas_call | solution.py:399
  40.8 1.1 %shard_map.94 = (bf16[128,2048]{1,0:T(8,128)(2,1)}, bf16[128,2048]{1,0:T(8,128)(2,1)}, bf16[128,512]{1,0:T(8,128)(2,1)}, bf16[128,512]{1,0:T(8,128)(2,1)}) custom-call(bf16[128,2048]{1,0:T(8,128)(2,1)S(1)} %get-tuple-element.8.refs_0_, bf16[128,2048]{1,0:T(8,128)(2,1)S(1)} %get-tuple-element.9.refs_1_, bf16[128,512]{1,0:T(8,128)(2,1)S(1)} %get-tuple-element.10.refs_2_, ...), custom_call_target="tpu_custom_call" | custom-call | tf_op jit(solution)/shard_map/pallas_call | solution.py:438

commit v4 on v3

--- a/solution.py
+++ b/solution.py
@@ -35,7 +35,7 @@
 def body(
     q_hbm, k_hbm, v_hbm, g_hbm, size_hbm, pad_hbm,
     o, dq, dk, dv,
-    q, g, kv, size_row, pad_row, meta, ex, dpr, stat,
+    q, g, kv, size_row, pad_row, meta, ex, dpr, stat, probs, dscores,
     t2, r2, u, ru, t1, t0,
     in_sem, f_send, f_recv, b_send, b_recv, m_send, m_recv,
 ):
@@ -97,10 +97,6 @@
         meta[pl.ds(dp, 1), 0:1, 0:16] = size_row[...].reshape(1, 1, 16)
         meta[pl.ds(dp, 1), 1:2, 0:16] = pad_row[...].reshape(1, 1, 16)
 
-    for group in loads:
-        group[0].wait()
-        group[2].wait()
-
     @pl.when(told)
     def _():
         pl.semaphore_wait(barrier, 1)
@@ -152,8 +148,6 @@
         for a, b in zip(own[h], relay[h]):
             a.wait_recv()
             b.start()
-
-    stacks = {}
 
     def part(h, at):
         rows = slice((2 - at) * ROWS, (3 - at) * ROWS)
@@ -211,22 +205,30 @@
         for c in own[h]:
             c.wait_send()
 
-    start(own[0])
-    start(own[1])
+    def send_own(h):
+        loads[h][0].wait()
+        loads[h][2].wait()
+        start(own[h])
+
+    send_own(0)
     wait_rest(0)
     part(0, 0)
     sent(0)
-    start(own[2])
-    exchange_x()
+    send_own(1)
     wait_rest(1)
     part(1, 0)
-    exchange_y()
+    sent(1)
+    send_own(2)
     wait_rest(2)
     part(2, 0)
-    sent(1)
+    exchange_x()
+    sent(2)
+    loads[3][0].wait()
+    loads[3][2].wait()
+    pl.when(ctx < CTX - 2)(lambda: start(own[3]))
     wait_rest(3)
     part(3, 0)
-    start(own[3])
+    exchange_y()
     relay_on(0)
 
     @pl.when(ctx == 0)
@@ -234,6 +236,7 @@
         table.wait_recv()
         table.start()
 
+    pl.when(ctx >= CTX - 2)(lambda: start(own[3]))
     relay_on(1)
     part(0, 1)
     relay_on(2)
@@ -288,14 +291,15 @@
         whole = sum(w[at] * stat[h, at, 1:2] for at in range(3))
         share = live / whole
         delta = sum(w[at] * stat[h, at, 2:3] for at in range(3)) * share
-        p16, ds16 = {}, {}
         for at in (2, 1, 0):
             rows = slice((2 - at) * ROWS, (3 - at) * ROWS)
             p = ex[h, rows] * (w[at] * share)
-            p16[at] = p.astype(jnp.bfloat16)
-            ds16[at] = (p * (dpr[h, rows] - delta)).astype(jnp.bfloat16)
-            dval = dot(p16[at], gs, (1, 0))
-            dkey = dot(ds16[at], qs, (1, 0))
+            p16 = p.astype(jnp.bfloat16)
+            ds16 = (p * (dpr[h, rows] - delta)).astype(jnp.bfloat16)
+            probs[h, rows] = p16
+            dscores[h, rows] = ds16
+            dval = dot(p16, gs, (1, 0))
+            dkey = dot(ds16, qs, (1, 0))
             if at == 2:
                 t2[1, h] = dval.astype(jnp.bfloat16)
                 send_back(0, h, 1)
@@ -305,15 +309,10 @@
                 keep = (t0, t1)[at]
                 keep[1, h] = dval
                 keep[0, h] = dkey
-        stacks[h] = (
-            jnp.concatenate([p16[2], p16[1], p16[0]], axis=0),
-            jnp.concatenate([ds16[2], ds16[1], ds16[0]], axis=0),
-        )
 
     def outputs(h):
-        p16, ds16 = stacks[h]
-        ot = dot(kv[1, h], p16, (0, 0))
-        qt = dot(kv[0, h], ds16, (0, 0)) * SCALE
+        ot = dot(kv[1, h], probs[h], (0, 0))
+        qt = dot(kv[0, h], dscores[h], (0, 0)) * SCALE
         for i in range(GROUP):
             at = slice(h * WIDE + i * D, h * WIDE + (i + 1) * D)
             o[:, at] = ot[:, i * D : (i + 1) * D].T.astype(jnp.bfloat16)
@@ -324,7 +323,6 @@
             c.wait_recv()
         part(h, 2)
         finish(h)
-        outputs(h)
 
     def middle(h):
         for i in (1, 0):
@@ -358,12 +356,16 @@
             middle_if(0, usual)
     middle_if(1, usual)
     middle_if(2, usual)
+    outputs(0)
+    outputs(1)
     middle_if(3, jnp.logical_not(second))
+    outputs(2)
+    outputs(3)
     for h in range(KV_HEADS):
         last(h)
 
     for h in range(KV_HEADS):
-        for c in (own[h] if h > 1 else []) + relay[h]:
+        for c in (own[h] if h == KV_HEADS - 1 else []) + relay[h]:
             c.wait_send()
         for stage in range(2):
             for i in range(2):
@@ -411,6 +413,8 @@
             pltpu.VMEM(scores, f32),
             pltpu.VMEM(scores, f32),
             pltpu.VMEM((KV_HEADS, 3, 8, WIDE), f32),
+            pltpu.VMEM(scores, bf16),
+            pltpu.VMEM(scores, bf16),
             pltpu.VMEM(terms, bf16),
             pltpu.VMEM(terms, bf16),
             pltpu.VMEM(terms, bf16),

time: 42.5 us -> 45 us (1.059)
  Pallas kernels: 41.3 us -> 44.2 us
    pallas_call x1, Pallas kernels: 40.2 us -> 43.1 us  [on_device(): pl.pallas_call(body, out_shape=tuple((jax.ShapeDtypeStruct(shape, bf16) f...]
where the time goes in v4:
time: 45 us; the launch traced here: 44.8 us
  Pallas kernels  44.2 us (98%)
  between operations  0.64 us (1%)
    pallas_call x1, Pallas kernels, on_device(): pl.pallas_call(body, out_shape=tuple((jax.ShapeDtypeStruct(shape, bf16) f...  43.1 us
    pallas_call x1, Pallas kernels, on_device(): pl.pallas_call(write_out, out_shape=tuple((jax.ShapeDtypeStruct(shape, bf...  1.08 us

profile of v4, /device:TPU:25, one launch (start us, length us, event | category | flops | bytes accessed | tf_op | source)
XLA Modules:
  0.0 44.8 jit_solution(18158217501922863478)
XLA Ops:
  0.6 43.1 %shard_map.93 = (bf16[128,2048]{1,0:T(8,128)(2,1)S(1)}, bf16[128,2048]{1,0:T(8,128)(2,1)S(1)}, bf16[128,512]{1,0:T(8,128)(2,1)S(1)}, bf16[128,512]{1,0:T(8,128)(2,1)S(1)}) custom-call(bf16[128,2048]{1,0:T(8,128)(2,1)} %q_hbm.1, bf16[128,512]{1,0:T(8,128)(2,1)} %k_hbm.1, bf16[128,512]{1,0:T(8,128)(2,1)} %v_hbm.1, bf16[128,2048]{1,0:T(8,128)(2,1)} %g_hbm.1, ...), custom_call_target="tpu_custom_call" | custom-call | tf_op jit(solution)/shard_map/pallas_call | solution.py:401
  43.7 1.1 %shard_map.94 = (bf16[128,2048]{1,0:T(8,128)(2,1)}, bf16[128,2048]{1,0:T(8,128)(2,1)}, bf16[128,512]{1,0:T(8,128)(2,1)}, bf16[128,512]{1,0:T(8,128)(2,1)}) custom-call(bf16[128,2048]{1,0:T(8,128)(2,1)S(1)} %get-tuple-element.8.refs_0_, bf16[128,2048]{1,0:T(8,128)(2,1)S(1)} %get-tuple-element.9.refs_1_, bf16[128,512]{1,0:T(8,128)(2,1)S(1)} %get-tuple-element.10.refs_2_, ...), custom_call_target="tpu_custom_call" | custom-call | tf_op jit(solution)/shard_map/pallas_call | solution.py:442
